TPU v7x, 32 devices: a whole 2x2x4 slice. The times are simulated.
32 devices in a mesh: groups: 2 (over y), ctx: 4 (over z), tp: 4 (over x, core).
Axes of the slice: x: 2, y: 2, z: 4, core: 2. Of those that a mesh axis runs over, the one named last changes fastest.
Arguments:
- streams: bfloat16 [3, 1024, 8192], P(None, ('groups', 'ctx'), 'tp'), parts along dimension 1, may hold values from -6 to 6
- short_filter: float32 [3, 3, 8192], P(None, None, 'tp'), may hold values from -3 to 3
- decay_rate: float32 [8192, 16], P('tp'), may hold values from 0 to 1
- residue: float32 [8192, 16], P('tp'), may hold values from -0.2 to 0.2
- skip_gain: float32 [8192], P('tp'), may hold values from -4 to 4
- lengths: int32 [4], P('groups'), parts along dimension 0, may hold values from 1 to 448, 512 in all
- queries: bfloat16 [1024, 8192], P(('groups', 'ctx'), 'tp'), parts along dimension 0, may hold values from -8 to 8
- keys: bfloat16 [1024, 8192], P(('groups', 'ctx'), 'tp'), parts along dimension 0, may hold values from -8 to 8
Outputs:
- hyena_out: bfloat16 [1024, 8192], P(('groups', 'ctx'), 'tp'), parts along dimension 0
- attended: bfloat16 [1024, 8192], P(('groups', 'ctx'), 'tp'), parts along dimension 0
There are 2 independent parts, one for each index of `groups`. A program takes and returns all parts, laid end to end along the dimension named above; an argument that names none is the same for every part. Nothing has to cross between parts.
Inputs may be any that keep to these rules, and one draw needn't show every extreme that they name: The requests fill the group in order, their lengths sum to 512, and the longest has at most 448 tokens.
All inputs are finite; a program needn't handle non-finite values.
Results may differ from a plain program's by a relative error of at most 0.01.
Values may be sent and summed in bfloat16 or wider, within the bound.
A program may use at most 128 MiB of HBM per device.

v0:
```python
import math

import jax
import jax.numpy as jnp
from jax import lax
from jax.sharding import PartitionSpec as P

HEAD_DIM = 128
SHORT = 3


def shifted(value, axis, steps):
    count = lax.axis_size(axis)
    leading, last = (max(0, -steps), min(count, count - steps))
    return lax.ppermute(value, axis, [(source, source + steps) for source in range(leading, last)])


def prefix(shard, axis, join, neutral):
    place = lax.axis_index(axis)
    gathered = jax.tree.map(
        lambda a, kind: lax.all_gather(a.astype(kind), axis),
        shard,
        (jnp.bfloat16, jnp.bfloat16, jnp.bfloat16),
    )
    state = jax.tree.map(lambda a, e: jnp.zeros_like(a) + jnp.asarray(e, a.dtype), shard, neutral)

    def one(step, state):
        return join(
            state,
            jax.tree.map(
                lambda a, own: lax.dynamic_index_in_dim(a, step, 0, False).astype(own.dtype),
                gathered,
                shard,
            ),
        )

    return lax.fori_loop(0, place, one, state)


def doc_of(places, ends):
    return jnp.sum((places[:, None] >= ends[None, :]).astype(jnp.int32), axis=1)


def shards(streams, short_filter, decay_rate, residue, skip_gain, lengths, queries, keys):
    rows = streams.shape[1]
    width = streams.shape[2]
    modes = decay_rate.shape[1]
    index = lax.axis_index("ctx")
    first = index * rows
    ends = jnp.cumsum(lengths)
    places = first + jnp.arange(rows, dtype=jnp.int32)
    doc_here = doc_of(places, ends)
    doc_before = doc_of(jnp.reshape(first - 1, (1,)), ends)[0]
    reach_back = SHORT - 1
    rim = shifted(streams[:, rows - reach_back :, :], "ctx", 1)
    extended = jnp.concatenate([rim, streams], axis=1)
    doc_ext = doc_of(first - reach_back + jnp.arange(rows + reach_back, dtype=jnp.int32), ends)
    filtered = jnp.zeros(streams.shape, jnp.float32)
    for tap in range(SHORT):
        window = extended[:, reach_back - tap : reach_back - tap + rows, :].astype(jnp.float32)
        same = (doc_ext[reach_back - tap : reach_back - tap + rows] == doc_here).astype(jnp.float32)
        filtered = filtered + short_filter[tap][:, None, :] * window * same[None, :, None]
    mixed = filtered[1] * filtered[2]
    sub_len = math.gcd(rows, 16)
    blocks = rows // sub_len
    lags = jnp.arange(sub_len + 1, dtype=jnp.float32)
    powers = jnp.exp(-decay_rate[None] * lags[:, None, None])
    kernel = jnp.sum(residue[None] * powers[:sub_len], axis=2)
    padded = jnp.concatenate([kernel[::-1], jnp.zeros_like(kernel)], axis=0)
    tiled = jnp.tile(padded, (sub_len, 1))[: sub_len * (2 * sub_len - 1)]
    toeplitz = tiled.reshape(sub_len, 2 * sub_len - 1, width)[:, sub_len - 1 :, :]
    mixed_blocks = mixed.reshape(blocks, sub_len, width)
    doc_blocks = doc_here.reshape(blocks, sub_len)
    same_blocks = (doc_blocks[:, :, None] == doc_blocks[:, None, :]).astype(jnp.float32)
    local = jnp.sum(toeplitz[None] * same_blocks[..., None] * mixed_blocks[:, None, :, :], axis=2)
    prior = jnp.concatenate([doc_before.reshape(1), doc_blocks[:-1, -1]])
    in_last = (doc_blocks == doc_blocks[:, -1:]).astype(jnp.float32)
    ahead = powers[sub_len:0:-1]
    summaries = jnp.einsum(
        "bjc,jcm->bcm", mixed_blocks * in_last[..., None], ahead, precision=lax.Precision.HIGHEST
    )
    keeps = (doc_blocks[:, -1] == prior).astype(jnp.float32)
    step_decay = powers[sub_len]

    def advance(carry, item):
        state, factor = carry
        summary, keep = item
        gain = step_decay * keep
        return ((state * gain + summary, factor * gain), (state, factor))

    empty_state = jnp.zeros((width, modes), jnp.float32)
    (own_state, own_factor), (pre_state, pre_factor) = lax.scan(
        advance, (empty_state, jnp.ones((width, modes), jnp.float32)), (summaries, keeps)
    )
    keep_device = jnp.prod(keeps)

    def combine(earlier, later):
        state_a, keep_a, count_a = earlier
        state_b, keep_b, count_b = later
        span = jnp.exp(-decay_rate * (rows * count_b))
        return (state_a * span * keep_b + state_b, keep_a * keep_b, count_a + count_b)

    incoming, keep_sum, count_sum = prefix(
        (own_state, keep_device, jnp.ones((), jnp.float32)),
        "ctx",
        combine,
        (empty_state, jnp.ones((), jnp.float32), jnp.zeros((), jnp.float32)),
    )
    starts = pre_state + pre_factor * incoming[None]
    carry_mask = (doc_blocks == prior[:, None]).astype(jnp.float32)
    cross = (
        jnp.einsum(
            "jcm,bcm->bjc",
            powers[:sub_len],
            residue[None] * starts,
            precision=lax.Precision.HIGHEST,
        )
        * carry_mask[..., None]
    )
    long = (local + cross).reshape(rows, width) + skip_gain[None, :] * mixed
    hyena_out = (filtered[0] * long).astype(jnp.bfloat16)
    heads_here = width // HEAD_DIM
    scale = 1.0 / math.sqrt(HEAD_DIM)
    query_docs = doc_of(places, ends)
    query_heads = queries.reshape(rows, heads_here, HEAD_DIM)
    paired = jnp.stack([keys, hyena_out])
    start_carry = (
        jnp.full((heads_here, rows), -1e30, jnp.float32),
        jnp.zeros((heads_here, rows), jnp.float32),
        jnp.zeros((heads_here, rows, HEAD_DIM), jnp.float32),
    )
    piece = lax.all_gather(paired, "ctx", axis=1, tiled=True)
    count = piece.shape[1]
    key_places = jnp.arange(count, dtype=jnp.int32)
    key_docs = doc_of(key_places, ends)
    allowed = (key_places[None, :] <= places[:, None]) & (key_docs[None, :] == query_docs[:, None])

    def compute(state):
        top, total, summed = state
        key_heads = piece[0].reshape(count, heads_here, HEAD_DIM)
        value_heads = piece[1].reshape(count, heads_here, HEAD_DIM)
        scores = jnp.einsum(
            "qhd,khd->hqk", query_heads, key_heads, preferred_element_type=jnp.float32
        )
        masked = jnp.where(allowed[None], scores * scale, -1e30)
        new_top = jnp.maximum(top, jnp.max(masked, axis=2))
        weight = jnp.exp(masked - new_top[..., None])
        total = jnp.sum(weight, axis=2)
        summed = jnp.einsum(
            "hqk,khd->hqd",
            weight.astype(jnp.bfloat16),
            value_heads,
            preferred_element_type=jnp.float32,
        )
        return (new_top, total, summed)

    def unchanged(state):
        return state

    result = lax.cond(jnp.any(allowed), compute, unchanged, start_carry)
    top, total, summed = result
    attended_rows = (
        (summed / total[..., None]).transpose(1, 0, 2).reshape(rows, width).astype(jnp.bfloat16)
    )
    return (hyena_out, attended_rows)


def solution(mesh):
    placed = (
        P(None, ("groups", "ctx"), "tp"),
        P(None, None, "tp"),
        P("tp", None),
        P("tp", None),
        P("tp"),
        P("groups"),
        P(("groups", "ctx"), "tp"),
        P(("groups", "ctx"), "tp"),
    )
    return jax.shard_map(
        shards,
        mesh=mesh,
        in_specs=placed,
        out_specs=(P(("groups", "ctx"), "tp"), P(("groups", "ctx"), "tp")),
        check_vma=False,
    )
```

profile of v0, /device:TPU:26, one launch (start us, length us, event | category | flops | bytes accessed | tf_op | source)
XLA Modules:
  0.0 345.3 jit_solution(5851390401221781662)
XLA Ops:
  7.2 1.5 slice.70
  8.7 1.3 collective-permute-start
  12.2 1.4 slice_bitcast_fusion.2
  14.9 11.2 %multiply_exponential_fusion = f32[17,2048,16]{2,0,1:T(8,128)} fusion(f32[2048,16]{1,0:T(8,128)S(1)} %copy.71), kind=kLoop, calls=%fused_computation.21 | loop fusion | flops 557056 | bytes 2359296 | tf_op jit(solution)/shard_map/exp | solution.py:67
  27.1 1.9 fusion.35
  29.0 20.8 %fusion.37 = (f32[16,2048,16]{2,0,1:T(8,128)}, f32[16,2048]{0,1:T(8,128)S(1)}) fusion(f32[17,2048,16]{2,0,1:T(8,128)} %multiply_exponential_fusion, f32[2048,16]{1,0:T(8,128)S(1)} %copy.70), kind=kLoop, calls=%fused_computation.78 | loop fusion | flops 1015808 | bytes 6553600 | tf_op jit(solution)/shard_map/slice | solution.py:78
  51.1 1.3 dynamic-update-slice.1
  53.0 10.2 %all-reduce.3 = (bf16[4]{0:T(256)(128)(2,1)}, bf16[4]{0:T(256)(128)(2,1)}) all-reduce(bf16[4]{0:T(256)(128)(2,1)S(1)} %dynamic-update-slice, bf16[4]{0:T(256)(128)(2,1)S(1)} %dynamic-update-slice.1), channel_id=1, replica_groups=mesh['groups'=2,'ctx'=4,'tp'=4] {'ctx'}, use_global_device_ids=true, to_apply=%add.1 | all-reduce | flops 8 | bytes 32
  63.3 3.8 %slice.97 = f32[1,2048,16]{2,0,1:T(1,128)S(1)} slice(f32[17,2048,16]{2,0,1:T(8,128)} %multiply_exponential_fusion), slice={[16:17], [0:2048], [0:16]} | slice | bytes 262144 | tf_op jit(solution)/shard_map/slice | solution.py:83
  67.0 1.4 rev.6
  69.3 2.2 slice.93
  71.5 3.7 %reshape.154 = f32[16,31,2048]{2,1,0:T(8,128)} reshape(f32[496,2048]{1,0:T(8,128)} %slice.93) | data formatting | bytes 8126464 | tf_op jit(solution)/shard_map/reshape | solution.py:71
  75.2 3.6 %slice.94 = f32[16,16,2048]{2,1,0:T(8,128)} slice(f32[16,31,2048]{2,1,0:T(8,128)} %reshape.154), slice={[0:16], [15:31], [0:2048]} | slice | bytes 4194304 | tf_op jit(solution)/shard_map/slice | solution.py:71
  79.8 22.3 %rev.7 = f32[16,2048,16]{2,0,1:T(8,128)} reverse(f32[16,2048,16]{2,0,1:T(8,128)} %get-tuple-element.333), dimensions={0} | reverse | bytes 4194304 | tf_op jit(solution)/shard_map/rev | solution.py:78
  102.0 3.7 %multiply_add_fusion = f32[3,128,2048]{2,1,0:T(8,128)S(1)} fusion(bf16[3,128,2048]{2,1,0:T(8,128)(2,1)} %param.14, bf16[3,2,2048]{2,1,0:T(2,128)(2,1)} %collective-permute-done, f32[128]{0:T(128)} %get-tuple-element.343, f32[3,2048]{1,0:T(4,128)} %get-tuple-element.336, f32[128]{0:T(128)} %get-tuple-element.344, f32[3,2048]{1,0:T(4,128)} %get-tuple-element.337, ...), kind=kLoop, calls=%fused_computation.30 | loop fusion | flops 13369344 | bytes 4818432 | tf_op jit(solution)/shard_map/add | solution.py:62
  105.8 1.1 slice_multiply_fusion
  106.9 5.9 %copy.73 = f32[8,16,2048]{1,0,2:T(8,128)} copy(f32[8,16,2048]{2,1,0:T(8,128)} %bitcast.87) | data formatting | bytes 2097152 | tf_op jit(solution)/shard_map/mul | solution.py:63
  112.8 20.2 %fusion.19 = f32[8,2048,16]{2,0,1:T(8,128)} fusion(f32[16,2048,16]{2,0,1:T(8,128)} %rev.7, f32[8,16,2048]{1,0,2:T(8,128)} %copy.73, f32[8,16]{1,0:T(8,128)S(1)} %get-tuple-element.339), kind=kOutput, calls=%fused_computation.29 | convolution fusion | flops 50593792 | bytes 4194816 | tf_op jit(solution)/shard_map/bjc,jcm->bcm/dot_general | solution.py:79
  133.1 6.0 %copy.75 = f32[8,2048,16]{1,2,0:T(8,128)} copy(f32[8,2048,16]{2,0,1:T(8,128)} %fusion.19) | data formatting | bytes 2097152
  139.1 24.3 %while.33 = (s32[]{:T(128)}, f32[2048,16]{0,1:T(8,128)S(1)}, f32[2048,16]{0,1:T(8,128)S(1)}, f32[8,2048,16]{1,2,0:T(8,128)}, f32[8,2048,16]{1,2,0:T(8,128)}, /*i...) while((s32[]{:T(128)}, f32[2048,16]{0,1:T(8,128)S(1)}, ...), condition=%wide.region_7.8_spmd.clone, body=%wide.region_6.7_spmd.clone.sunk | while | flops 262147 | bytes 1310864 | solution.py:92
  140.4 1.7 select_multiply_fusion.2
  143.4 1.7 select_multiply_fusion.2
  146.5 1.7 select_multiply_fusion.2
  149.5 1.7 select_multiply_fusion.2
  152.6 1.7 select_multiply_fusion.2
  155.6 1.7 select_multiply_fusion.2
  158.7 1.7 select_multiply_fusion.2
  161.7 1.7 select_multiply_fusion.2
  163.4 14.4 %all-gather = bf16[8192,16]{0,1:T(8,128)(2,1)S(1)} all-gather(bf16[2048,16]{0,1:T(8,128)(2,1)S(1)} %convert_element_type.129), channel_id=2, replica_groups=mesh['groups'=2,'ctx'=4,'tp'=4] {'ctx'}, dimensions={0}, use_global_device_ids=true | all-gather | bytes 327680 | tf_op jit(solution)/shard_map/all_gather | solution.py:21
  178.6 12.4 %while.32 = (s32[]{:T(128)}, f32[2048,16]{0,1:T(8,128)S(1)}, s32[]{:T(128)}, bf16[4]{0:T(256)(128)(2,1)S(1)}, f32[2048,16]{0,1:T(8,128)S(1)}, /*index=5*/bf16[4]...) while((s32[]{:T(128)}, f32[2048,16]{0,1:T(8,128)S(1)}, ...), condition=%wide.region_10.11_spmd, body=%wide.region_9.10_spmd.sunk | while | flops 163847 | bytes 458947 | solution.py:37
  178.6 1.2 dynamic_slice.37
  182.6 1.2 dynamic_slice.37
  186.7 1.2 dynamic_slice.37
  191.0 2.7 add_multiply_fusion
  193.6 5.9 %copy.77 = f32[8,2048,16]{2,0,1:T(8,128)} copy(f32[8,2048,16]{1,2,0:T(8,128)} %add_multiply_fusion) | data formatting | bytes 2097152 | tf_op jit(solution)/shard_map/mul | solution.py:115
  199.6 30.8 %fusion.14 = f32[2048,8,16]{2,1,0:T(8,128)} fusion(f32[8,2048,16]{2,0,1:T(8,128)} %copy.77, f32[17,2048,16]{2,0,1:T(8,128)} %multiply_exponential_fusion), kind=kOutput, calls=%fused_computation.24 | convolution fusion | flops 50331648 | bytes 26214400 | tf_op jit(solution)/shard_map/jcm,bcm->bjc/dot_general | solution.py:112
  230.4 6.0 %copy.78 = f32[2048,8,16]{0,2,1:T(8,128)} copy(f32[2048,8,16]{2,1,0:T(8,128)} %fusion.14) | data formatting | bytes 2097152 | tf_op jit(solution)/shard_map/jcm,bcm->bjc/dot_general | solution.py:112
  236.5 6.5 %multiply_reduce_fusion = f32[8,16,2048]{2,1,0:T(8,128)S(1)} fusion(f32[8,16,2048]{2,1,0:T(8,128)} %bitcast.88, f32[8,16,16]{2,1,0:T(8,128)S(1)} %copy-done.5, f32[16,16,2048]{2,1,0:T(8,128)} %slice.94), kind=kLoop, calls=%fused_computation.22 | loop fusion | flops 12320768 | bytes 4202496 | tf_op jit(solution)/shard_map/reduce_sum | solution.py:75
  244.5 1.1 pad_maximum_fusion.1
  247.1 2.3 fusion.27
  249.4 75.5 %all-gather.3.cloned.1.call-done = bf16[2,512,2048]{2,1,0:T(8,128)(2,1)} async-done(((bf16[2,128,2048]{2,1,0:T(8,128)(2,1)}), bf16[2,512,2048]{2,1,0:T(8,128)(2,1)}) %all-gather.3.cloned.1.call-update) | async-done | bytes 4194320 | tf_op jit(solution)/shard_map/all_gather | solution.py:132
  325.0 12.3 %conditional.1 = (f32[16,128]{1,0:T(8,128)S(1)}, f32[16,128,128]{2,1,0:T(8,128)S(1)}) conditional(s32[]{:T(128)} %convert_element_type.133, () %tuple.36, (pred[128,512]{1,0:T(8,128)(4,1)S(1)}, bf16[128,2048]{1,0:T(8,128)(2,1)}, bf16[2,512,2048]{2,1,0:T(8,128)(2,1)}) %tuple.37), branch_computations={%region_13.14_spmd, %region_14.17_spmd} | conditional | flops 548403200 | bytes 37470252 | solution.py:160
  325.0 6.2 %copy.79 = bf16[2,512,2048]{1,2,0:T(8,128)(2,1)} copy(bf16[2,512,2048]{2,1,0:T(8,128)(2,1)} %get-tuple-element.289) | data formatting | bytes 8388608 | tf_op jit(solution)/shard_map
  331.2 2.6 fusion.36
  333.8 1.0 fusion
  334.7 1.3 fusion.2
  336.0 1.2 fusion.3
  337.3 1.1 copy_bitcast_fusion
  (88 shorter events, 26.5 us)
Async XLA Ops:
  7.2 317.8 %all-gather.3.cloned.1.call-start = ((), (), s32[]{:S(2)}) async-start(), calls=%async_computation | async-start | bytes 5242880 | tf_op jit(solution)/shard_map/all_gather | solution.py:132
  8.7 93.3 %collective-permute-start = (bf16[3,2,2048]{2,1,0:T(2,128)(2,1)}, bf16[3,2,2048]{2,1,0:T(2,128)(2,1)}, u32[]{:S(2)}, u32[]{:S(2)}) collective-permute-start(bf16[3,2,2048]{2,1,0:T(2,128)(2,1)} %slice.70), channel_id=1, source_target_pairs={{0,4},{4,8},{8,12},{1,5},{5,9},{9,13},{2,6},{6,10},{10,14},{3,7},{... | collective-permute-start | bytes 73736 | tf_op jit(solution)/shard_map/ppermute | solution.py:15
  10.0 1.7 copy-start.9
  10.9 15.6 %copy-start.7 = (s32[2,1]{0,1:T(1,128)}, s32[2,1]{0,1:T(1,128)S(1)}, u32[]{:S(2)}) copy-start(s32[2,1]{0,1:T(1,128)S(1)} %reduce-window.4) | copy-start | bytes 28
  14.9 11.2 %copy-start.4 = (f32[2048,16]{0,1:T(8,128)S(1)}, f32[2048,16]{0,1:T(8,128)}, u32[]{:S(2)}) copy-start(f32[2048,16]{0,1:T(8,128)} %param.17) | copy-start | bytes 393220
  29.0 20.8 %copy-start.13 = (u32[32]{0:T(128)S(1)}, u32[32]{0:T(128)}, u32[]{:S(2)}) copy-start(u32[32]{0:T(128)} %constant.86) | copy-start | bytes 388
  133.1 6.0 %copy-start.11 = (f32[8]{0:T(128)S(1)}, f32[8]{0:T(128)}, u32[]{:S(2)}) copy-start(f32[8]{0:T(128)} %get-tuple-element.451) | copy-start | bytes 100
  139.1 39.5 %copy-start.12 = (bf16[4]{0:T(256)(128)(2,1)S(1)}, bf16[4]{0:T(256)(128)(2,1)}, u32[]{:S(2)}) copy-start(bf16[4]{0:T(256)(128)(2,1)} %get-tuple-element.479) | copy-start | bytes 28
  230.4 6.0 %copy-start.5 = (f32[8,16,16]{2,1,0:T(8,128)S(1)}, f32[8,16,16]{2,1,0:T(8,128)}, u32[]{:S(2)}) copy-start(f32[8,16,16]{2,1,0:T(8,128)} %compare_convert_fusion) | copy-start | bytes 24580
  236.4 6.5 %copy-start.1 = (f32[2048,8,16]{0,2,1:T(8,128)S(1)}, f32[2048,8,16]{0,2,1:T(8,128)}, u32[]{:S(2)}) copy-start(f32[2048,8,16]{0,2,1:T(8,128)} %copy.78) | copy-start | bytes 3145732
  236.5 7.7 %copy-start.6 = (f32[2048]{0:T(1024)S(1)}, f32[2048]{0:T(1024)}, u32[]{:S(2)}) copy-start(f32[2048]{0:T(1024)} %param.18) | copy-start | bytes 24580
  242.9 1.5 copy-start.2
  243.1 1.0 copy-start
  243.1 2.4 copy-start.8
  243.2 2.5 copy-start.10
  331.2 2.6 copy-start.3
Sparse Core Ops, SparseCore 0:
  245.7 79.2 all-gather.2
where the time goes:
time: 351 us; the launch traced here: 345 us
  local copies, waits for them, and re-layouts  90.2 us (26%)
  other arithmetic  81.1 us (23%)
  waiting for transfers between devices  75.6 us (22%)
  matrix products  53.2 us (15%)
  blocking collectives  24.6 us (7%)
  between operations  14.9 us (4%)
  loops' own time  4.31 us (1%)
    all_gather x1, waiting for transfers between devices, shards(): piece = lax.all_gather(paired, 'ctx', axis=1, tiled=True)  75.5 us
    dot_general x1, matrix products, shards(): jnp.einsum('jcm,bcm->bjc', powers[:sub_len], residue[None] * starts, prec...  30.8 us
    rev x1, local copies, waits for them, and re-layouts, shards(): ahead = powers[sub_len:0:-1]  22.3 us
    slice x1, other arithmetic, shards(): ahead = powers[sub_len:0:-1]  20.8 us
    dot_general x1, matrix products, shards(): jnp.einsum('bjc,jcm->bcm', mixed_blocks * in_last[..., None], ahead, prec...  20.2 us
    all_gather x1, blocking collectives, prefix(): lax.all_gather(a.astype(kind), axis)  14.4 us
    mul x8, other arithmetic, advance(): return ((state * gain + summary, factor * gain), (state, factor))  13.6 us
    unnamed x35, local copies, waits for them, and re-layouts  11.3 us
  transfers between devices with their start and end apart: 2, of which 1 were waited for; matrix products, arithmetic and copies ran while one was open for 25% of the time, Pallas kernels for 0%

commit v1 on v0

--- a/solution.py
+++ b/solution.py
@@ -1,8 +1,11 @@
+import functools
 import math
 
 import jax
 import jax.numpy as jnp
 from jax import lax
+from jax.experimental import pallas as pl
+from jax.experimental.pallas import tpu as pltpu
 from jax.sharding import PartitionSpec as P
 
 HEAD_DIM = 128
@@ -165,6 +168,430 @@
     return (hyena_out, attended_rows)
 
 
+LANES = 128
+SEGS = 8
+PARTS = 4
+NEG = -1e30
+DIMS = (((1,), (1,)), ((), ()))
+
+
+def fused_kernel(
+    lengths, streams, taps, rate, residue, skip, queries, keys, hyena, attended,
+    ext, rim_out, rim_in, same, mixed_seg, gate_seg, starts, own, own_low, state_in, incoming,
+    tokens, query_in, key_in, value_in, part_out, part_in, lse_out, lse_in, own_part, lse_rows, bias,
+    rim_s, rim_r, state_s, state_r, query_s, query_r, key_s, key_r, value_s, value_r,
+    part_s, part_r, lse_s, lse_r,
+):
+    me = lax.axis_index("ctx")
+    rows, width = queries.shape
+    heads = width // LANES
+    modes = rate.shape[0]
+    seg = rows // SEGS
+    group = width // PARTS
+    per = heads // PARTS
+    first = me * rows
+
+    def send(src, dst, s, r, to):
+        return pltpu.make_async_remote_copy(
+            src_ref=src, dst_ref=dst, send_sem=s, recv_sem=r,
+            device_id={"ctx": to}, device_id_type=pl.DeviceIdType.MESH,
+        )
+
+    def cols(g):
+        return pl.ds(g * group, group)
+
+    def rim_copy(to):
+        return send(rim_out, rim_in, rim_s, rim_r, to)
+
+    def state_copy(source, to):
+        return send(own_low, state_in.at[source], state_s.at[to], state_r.at[source], to)
+
+    def query_copy(slot, g, to):
+        return send(
+            queries.at[:, cols(g)], query_in.at[slot, :, cols(g)],
+            query_s.at[to, g], query_r.at[slot, g], to,
+        )
+
+    def key_copy(g):
+        return send(keys.at[:, cols(g)], key_in.at[:, cols(g)], key_s.at[g], key_r.at[g], 1)
+
+    def value_copy(g):
+        return send(hyena.at[:, cols(g)], value_in.at[:, cols(g)], value_s.at[g], value_r.at[g], 1)
+
+    def part_copy(slot, source, g, to):
+        return send(
+            part_out.at[slot, :, cols(g)], part_in.at[source - 1, :, cols(g)],
+            part_s.at[slot, g], part_r.at[source - 1, g], to,
+        )
+
+    def lse_copy(slot, source, to):
+        return send(lse_out.at[slot], lse_in.at[source - 1], lse_s.at[slot], lse_r.at[source - 1], to)
+
+    barrier = pltpu.get_barrier_semaphore()
+    for away in range(1, 4):
+        pl.semaphore_signal(
+            barrier, inc=1, device_id={"ctx": lax.rem(me + away, 4)},
+            device_id_type=pl.DeviceIdType.MESH,
+        )
+    for j in range(3):
+        rim_out[2 * j : 2 * j + 2, :] = streams[j, rows - 16 :, :].astype(jnp.float32)[14:16]
+    rim_out[6:8, :] = jnp.zeros((2, width), jnp.float32)
+    pl.semaphore_wait(barrier, 3)
+
+    for i in range(3):
+        @pl.when(me == i)
+        def _():
+            rim_copy(i + 1).start()
+
+    @pl.when(me == 0)
+    def _():
+        for g in range(PARTS):
+            key_copy(g).start()
+
+    @pl.when(me == 2)
+    def _():
+        for g in range(PARTS):
+            query_copy(0, g, 1).start()
+
+    @pl.when(me == 3)
+    def _():
+        for g in range(PARTS):
+            query_copy(1, g, 1).start()
+            query_copy(1, g, 2).start()
+
+    ends = []
+    total = jnp.int32(0)
+    for r in range(lengths.shape[0]):
+        total = total + lengths[r]
+        ends.append(total)
+
+    def doc(places):
+        found = jnp.zeros(places.shape, jnp.int32)
+        for end in ends:
+            found = found + (places >= end).astype(jnp.int32)
+        return found
+
+    def equal(a, b):
+        return (doc(a) == doc(b)).astype(jnp.float32)
+
+    segment = lax.broadcasted_iota(jnp.int32, (SEGS, LANES), 0)
+    for t in range(seg):
+        at = first + segment * seg + t
+        same[0, t] = equal(at, at - 1)
+        same[1, t] = equal(at, at - 2)
+    last = first + segment * seg + (seg - 1)
+    windows = [
+        equal(last, last - span * seg) * (segment >= span).astype(jnp.float32) for span in (1, 2, 4)
+    ]
+    before = segment * 0 + (first - 1)
+    carried = equal(first + segment * seg - 1, before)
+
+    def widen(h, _):
+        lanes = pl.ds(pl.multiple_of(h * LANES, LANES), LANES)
+        for j in range(3):
+            ext[j, h, 8:, :] = streams[j, :, lanes].astype(jnp.float32)
+        return _
+
+    lax.fori_loop(0, heads, widen, 0)
+
+    @pl.when(me == 0)
+    def _():
+        rim_in[...] = jnp.zeros(rim_in.shape, jnp.float32)
+
+    for i in range(1, 4):
+        @pl.when(me == i)
+        def _():
+            rim_copy(i - 1).wait_recv()
+
+    def spread(value):
+        return jnp.broadcast_to(value[:, None, :], (modes, SEGS, LANES))
+
+    def forward(h, _):
+        lanes = pl.ds(pl.multiple_of(h * LANES, LANES), LANES)
+        for j in range(3):
+            ext[j, h, 6:8, :] = rim_in[2 * j : 2 * j + 2, lanes]
+        speed = rate[:, lanes]
+        decay = spread(jnp.exp(-speed))
+        gains = [
+            [jnp.broadcast_to(taps[i, j : j + 1, lanes], (SEGS, LANES)) for j in range(3)]
+            for i in range(3)
+        ]
+        older = [ext[j, h, pl.ds(6, SEGS, stride=seg), :] for j in range(3)]
+        newer = [ext[j, h, pl.ds(7, SEGS, stride=seg), :] for j in range(3)]
+        state = jnp.zeros((modes, SEGS, LANES), jnp.float32)
+        for t in range(seg):
+            here = [ext[j, h, pl.ds(8 + t, SEGS, stride=seg), :] for j in range(3)]
+            near, far = same[0, t], same[1, t]
+            out = [
+                gains[0][j] * here[j] + gains[1][j] * (newer[j] * near) + gains[2][j] * (older[j] * far)
+                for j in range(3)
+            ]
+            mixed = out[1] * out[2]
+            gate_seg[h, t] = out[0]
+            mixed_seg[h, t] = mixed
+            state = state * near[None] * decay + mixed[None]
+            older, newer = newer, here
+        for window, span in zip(windows, (1, 2, 4)):
+            step = spread(jnp.exp(-speed * float(span * seg)))
+            state = state + step * window[None] * pltpu.roll(state, span, 1)
+        for m in range(modes):
+            own[m : m + 1, lanes] = state[m, SEGS - 1 :, :]
+        starts[h] = pltpu.roll(state, 1, 1) * (segment >= 1).astype(jnp.float32)[None]
+        return _
+
+    lax.fori_loop(0, heads, forward, 0)
+    own_low[...] = own[...].astype(jnp.bfloat16)
+    for i in range(3):
+        @pl.when(me == i)
+        def _():
+            for to in range(i + 1, 4):
+                state_copy(i, to).start()
+
+    incoming[...] = jnp.zeros(incoming.shape, jnp.float32)
+    edge = jnp.zeros((1, LANES), jnp.int32)
+    for i in range(1, 4):
+        @pl.when(me == i)
+        def _():
+            for j in range(i - 1, -1, -1):
+                state_copy(j, i).wait_recv()
+                linked = equal(edge + (j + 1) * rows - 1, edge + i * rows - 1)
+                linked = jnp.concatenate([linked] * heads, axis=1)
+                span = jnp.exp(-rate[...] * float(rows * (i - 1 - j))) * linked
+                incoming[...] = incoming[...] + state_in[j].astype(jnp.float32) * span
+
+    age = (segment * seg).astype(jnp.float32)
+
+    def backward(h, _):
+        lanes = pl.ds(pl.multiple_of(h * LANES, LANES), LANES)
+        speed = spread(rate[:, lanes])
+        decay = jnp.exp(-speed)
+        weight = spread(residue[:, lanes])
+        direct = jnp.broadcast_to(skip[:, lanes], (SEGS, LANES))
+        state = starts[h] + spread(incoming[:, lanes]) * (jnp.exp(-speed * age[None]) * carried[None])
+        for t in range(seg):
+            mixed = mixed_seg[h, t]
+            state = state * same[0, t][None] * decay + mixed[None]
+            long = jnp.sum(weight * state, axis=0) + direct * mixed
+            tokens[pl.ds(t, SEGS, stride=seg), :] = gate_seg[h, t] * long
+        hyena[:, lanes] = tokens[...].astype(jnp.bfloat16)
+        return _
+
+    for g in range(PARTS):
+        lax.fori_loop(g * per, (g + 1) * per, backward, 0)
+
+        @pl.when(me == 0)
+        def _():
+            value_copy(g).start()
+
+    scale = 1.0 / math.sqrt(HEAD_DIM)
+    lane = lax.broadcasted_iota(jnp.int32, (rows, LANES), 1)
+    down = lax.broadcasted_iota(jnp.int32, (rows, rows), 0)
+    across = lax.broadcasted_iota(jnp.int32, (rows, rows), 1)
+    lse_rows[...] = jnp.zeros(lse_rows.shape, jnp.float32)
+
+    def set_bias(query_block, key_block, a, b):
+        p = query_block * rows + down
+        q = key_block * rows + across
+        allowed = (q <= p) & (doc(p) == doc(q))
+        bias[a * rows : (a + 1) * rows, b * rows : (b + 1) * rows] = jnp.where(allowed, 0.0, NEG)
+
+    def attend(query, key, value, penalty):
+        scores = lax.dot_general(query, key, DIMS, preferred_element_type=jnp.float32)
+        scores = scores * scale + penalty
+        top = jnp.max(scores, axis=1, keepdims=True)
+        weight = jnp.exp(scores - top)
+        total = jnp.sum(weight, axis=1, keepdims=True)
+        summed = jnp.dot(weight.astype(jnp.bfloat16), value, preferred_element_type=jnp.float32)
+        return summed * (1.0 / total), top + jnp.log(total)
+
+    def note(slot, h, value):
+        lse_rows[slot] = jnp.where(lane == h, value, lse_rows[slot])
+
+    def head_lanes(h):
+        return pl.ds(pl.multiple_of(h * LANES, LANES), LANES)
+
+    def combine(sources):
+        tables = [lse_rows[0]]
+        for source in sources:
+            lse_copy(0, source, 0).wait_recv()
+            filler = jnp.zeros((LANES - heads, rows), jnp.float32)
+            tables.append(jnp.concatenate([lse_in[source - 1], filler], axis=0).T)
+        peak = functools.reduce(jnp.maximum, tables)
+        shares = [jnp.exp(table - peak) for table in tables]
+        norm = 1.0 / functools.reduce(jnp.add, shares)
+        shares = [share * norm for share in shares]
+        for g in range(PARTS):
+            for source in sources:
+                part_copy(0, source, g, 0).wait_recv()
+            for h in range(g * per, (g + 1) * per):
+                at = slice(h * LANES, (h + 1) * LANES)
+                whole = own_part[:, at] * shares[0][:, h : h + 1]
+                for share, source in zip(shares[1:], sources):
+                    whole = whole + part_in[source - 1, :, at].astype(jnp.float32) * share[:, h : h + 1]
+                attended[:, at] = whole.astype(jnp.bfloat16)
+
+    @pl.when(me == 0)
+    def _():
+        set_bias(0, 0, 0, 0)
+
+        def one(h, _):
+            at = head_lanes(h)
+            out, lse = attend(queries[:, at], keys[:, at], hyena[:, at], bias[:rows, :rows])
+            attended[:, at] = out.astype(jnp.bfloat16)
+            return _
+
+        lax.fori_loop(0, heads, one, 0)
+        for g in range(PARTS):
+            key_copy(g).wait_send()
+            value_copy(g).wait_send()
+
+    @pl.when(me == 1)
+    def _():
+        for a in range(3):
+            for b in range(2):
+                set_bias(a + 1, b, a, b)
+
+        def one(h, _):
+            at = head_lanes(h)
+            query = jnp.concatenate([query_in[0, :, at], query_in[1, :, at], queries[:, at]], axis=0)
+            key = jnp.concatenate([key_in[:, at], keys[:, at]], axis=0)
+            value = jnp.concatenate([value_in[:, at], hyena[:, at]], axis=0)
+            penalty = jnp.concatenate([bias[rows:, :], bias[:rows, :]], axis=0)
+            out, lse = attend(query, key, value, penalty)
+            part_out[0, :, at] = out[:rows].astype(jnp.bfloat16)
+            part_out[1, :, at] = out[rows : 2 * rows].astype(jnp.bfloat16)
+            attended[:, at] = out[2 * rows :].astype(jnp.bfloat16)
+            note(0, h, lse[:rows])
+            note(1, h, lse[rows : 2 * rows])
+            return _
+
+        for g in range(PARTS):
+            query_copy(0, g, 1).wait_recv()
+            query_copy(1, g, 1).wait_recv()
+            key_copy(g).wait_recv()
+            value_copy(g).wait_recv()
+            lax.fori_loop(g * per, (g + 1) * per, one, 0)
+            part_copy(0, 1, g, 2).start()
+            part_copy(1, 1, g, 3).start()
+        for slot in range(2):
+            lse_out[slot] = lse_rows[slot].T[:heads]
+            lse_copy(slot, 1, slot + 2).start()
+        for slot in range(2):
+            for g in range(PARTS):
+                part_copy(slot, 1, g, slot + 2).wait_send()
+            lse_copy(slot, 1, slot + 2).wait_send()
+
+    @pl.when(me == 2)
+    def _():
+        set_bias(3, 2, 0, 0)
+        set_bias(2, 2, 1, 0)
+
+        def one(h, _):
+            at = head_lanes(h)
+            query = jnp.concatenate([query_in[1, :, at], queries[:, at]], axis=0)
+            out, lse = attend(query, keys[:, at], hyena[:, at], bias[: 2 * rows, :rows])
+            part_out[0, :, at] = out[:rows].astype(jnp.bfloat16)
+            own_part[:, at] = out[rows:]
+            note(1, h, lse[:rows])
+            note(0, h, lse[rows:])
+            return _
+
+        for g in range(PARTS):
+            query_copy(1, g, 2).wait_recv()
+            lax.fori_loop(g * per, (g + 1) * per, one, 0)
+            part_copy(0, 2, g, 3).start()
+        lse_out[0] = lse_rows[1].T[:heads]
+        lse_copy(0, 2, 3).start()
+        combine((1,))
+        for g in range(PARTS):
+            query_copy(0, g, 1).wait_send()
+            part_copy(0, 2, g, 3).wait_send()
+        lse_copy(0, 2, 3).wait_send()
+
+    @pl.when(me == 3)
+    def _():
+        set_bias(3, 3, 0, 0)
+
+        def one(h, _):
+            at = head_lanes(h)
+            out, lse = attend(queries[:, at], keys[:, at], hyena[:, at], bias[:rows, :rows])
+            own_part[:, at] = out
+            note(0, h, lse)
+            return _
+
+        lax.fori_loop(0, heads, one, 0)
+        combine((2, 1))
+        for g in range(PARTS):
+            query_copy(1, g, 1).wait_send()
+            query_copy(1, g, 2).wait_send()
+
+    for i in range(3):
+        @pl.when(me == i)
+        def _():
+            rim_copy(i + 1).wait_send()
+            for to in range(i + 1, 4):
+                state_copy(i, to).wait_send()
+
+
+def fused(streams, short_filter, decay_rate, residue, skip_gain, lengths, queries, keys):
+    rows, width = queries.shape
+    heads = width // LANES
+    modes = decay_rate.shape[1]
+    seg = rows // SEGS
+    f32, bf16 = jnp.float32, jnp.bfloat16
+    vmem, dma = pltpu.VMEM, pltpu.SemaphoreType.DMA
+    block = pl.BlockSpec(memory_space=pltpu.VMEM)
+    out = jax.ShapeDtypeStruct((rows, width), bf16)
+    return pl.pallas_call(
+        fused_kernel,
+        out_shape=(out, out),
+        in_specs=[pl.BlockSpec(memory_space=pltpu.SMEM)] + [block] * 7,
+        out_specs=(block, block),
+        scratch_shapes=[
+            vmem((3, heads, rows + 8, LANES), f32),
+            vmem((8, width), f32),
+            vmem((8, width), f32),
+            vmem((2, seg, SEGS, LANES), f32),
+            vmem((heads, seg, SEGS, LANES), f32),
+            vmem((heads, seg, SEGS, LANES), f32),
+            vmem((heads, modes, SEGS, LANES), f32),
+            vmem((modes, width), f32),
+            vmem((modes, width), bf16),
+            vmem((3, modes, width), bf16),
+            vmem((modes, width), f32),
+            vmem((rows, LANES), f32),
+            vmem((2, rows, width), bf16),
+            vmem((rows, width), bf16),
+            vmem((rows, width), bf16),
+            vmem((2, rows, width), bf16),
+            vmem((2, rows, width), bf16),
+            vmem((2, heads, rows), f32),
+            vmem((2, heads, rows), f32),
+            vmem((rows, width), f32),
+            vmem((2, rows, LANES), f32),
+            vmem((3 * rows, 2 * rows), f32),
+            dma, dma, dma((4,)), dma((3,)), dma((4, PARTS)), dma((2, PARTS)),
+            dma((PARTS,)), dma((PARTS,)), dma((PARTS,)), dma((PARTS,)),
+            dma((2, PARTS)), dma((2, PARTS)), dma((2,)), dma((2,)),
+        ],
+        compiler_params=pltpu.CompilerParams(
+            collective_id=0, has_side_effects=True, vmem_limit_bytes=48 * 1024 * 1024
+        ),
+        cost_estimate=pl.CostEstimate(
+            flops=12 * rows * rows * width, bytes_accessed=14 * rows * width, transcendentals=0
+        ),
+    )(
+        lengths, streams, short_filter, decay_rate.T, residue.T, skip_gain.reshape(1, width),
+        queries, keys,
+    )
+
+
+def chosen(streams, *rest):
+    if lax.axis_size("ctx") == 4 and streams.shape[1] == 128 and streams.shape[2] % 512 == 0:
+        return fused(streams, *rest)
+    return shards(streams, *rest)
+
+
 def solution(mesh):
     placed = (
         P(None, ("groups", "ctx"), "tp"),
@@ -177,7 +604,7 @@
         P(("groups", "ctx"), "tp"),
     )
     return jax.shard_map(
-        shards,
+        chosen,
         mesh=mesh,
         in_specs=placed,
         out_specs=(P(("groups", "ctx"), "tp"), P(("groups", "ctx"), "tp")),

time: 351 us -> 61.7 us (0.18); the launches traced: 345 us -> 61.3 us
  other arithmetic: 81.1 us -> 0 us
  local copies, waits for them, and re-layouts: 90.2 us -> 9.12 us
  waiting for transfers between devices: 75.6 us -> 0 us
  matrix products: 53.2 us -> 0 us
  Pallas kernels: 0 us -> 51.5 us
  blocking collectives: 24.6 us -> 0 us
  between operations: 14.9 us -> 0.66 us
  loops' own time: 4.31 us -> 0 us
    all_gather x1 -> x0, waiting for transfers between devices: 75.5 us -> none  [shards(): piece = lax.all_gather(paired, 'ctx', axis=1, tiled=True)]
    dot_general x4 -> x0, matrix products: 53.2 us -> none  [the longest x1 30.8 us: shards(): jnp.einsum('jcm,bcm->bjc', powers[:sub_len], residue[None] * starts, prec...]
    pallas_call x0 -> x1, Pallas kernels: none -> 51.5 us  [fused(): pl.pallas_call(fused_kernel, out_shape=(out, out), in_specs=[pl.BlockSpec...]
    rev x2 -> x0, local copies, waits for them, and re-layouts: 23.7 us -> none  [the longest x1 22.3 us: shards(): ahead = powers[sub_len:0:-1]]
    slice x1 -> x0, other arithmetic: 20.8 us -> none  [shards(): ahead = powers[sub_len:0:-1]]
    mul x10 -> x0, other arithmetic: 17.4 us -> none  [the longest x8 13.6 us: advance(): return ((state * gain + summary, factor * gain), (state, factor))]
    all_gather x1 -> x0, blocking collectives: 14.4 us -> none  [prefix(): lax.all_gather(a.astype(kind), axis)]
    slice x7 -> x0, local copies, waits for them, and re-layouts: 14 us -> none  [the longest x1 3.75 us: shards(): step_decay = powers[sub_len]]
  transfers between devices with their start and end apart: 2 -> 0, of which waited for: 1 -> 0; matrix products, arithmetic and copies ran while one was open for 25% -> 0% of each run, Pallas kernels for 0% -> 0%
where the time goes in v1:
time: 61.7 us; the launch traced here: 61.3 us
  Pallas kernels  51.5 us (83%)
  local copies, waits for them, and re-layouts  9.12 us (15%)
  between operations  0.66 us (1%)
    pallas_call x1, Pallas kernels, fused(): pl.pallas_call(fused_kernel, out_shape=(out, out), in_specs=[pl.BlockSpec...  51.5 us
    unnamed x18, local copies, waits for them, and re-layouts  9.12 us

profile of v1, /device:TPU:26, one launch (start us, length us, event | category | flops | bytes accessed | tf_op | source)
XLA Modules:
  0.0 61.3 jit_solution(1746662810004909569)
XLA Ops:
  0.6 0.0 copy-start
  0.6 1.4 %copy-done = bf16[3,128,2048]{2,1,0:T(8,128)(2,1)S(1)} copy-done((bf16[3,128,2048]{2,1,0:T(8,128)(2,1)S(1)}, bf16[3,128,2048]{2,1,0:T(8,128)(2,1)}, u32[]{:S(2)}) %copy-start) | copy-done | bytes 1572888
  2.0 0.0 copy-start.1
  2.0 1.0 %copy-done.1 = bf16[128,2048]{1,0:T(8,128)(2,1)S(1)} copy-done((bf16[128,2048]{1,0:T(8,128)(2,1)S(1)}, bf16[128,2048]{1,0:T(8,128)(2,1)}, u32[]{:S(2)}) %copy-start.1) | copy-done | bytes 524312
  3.1 0.0 copy-start.2
  3.1 1.0 %copy-done.2 = bf16[128,2048]{1,0:T(8,128)(2,1)S(1)} copy-done((bf16[128,2048]{1,0:T(8,128)(2,1)S(1)}, bf16[128,2048]{1,0:T(8,128)(2,1)}, u32[]{:S(2)}) %copy-start.2) | copy-done | bytes 524312
  4.1 0.0 copy-start.3
  4.1 0.9 %copy-done.3 = f32[2048,16]{0,1:T(8,128)S(1)} copy-done((f32[2048,16]{0,1:T(8,128)S(1)}, f32[2048,16]{0,1:T(8,128)}, u32[]{:S(2)}) %copy-start.3) | copy-done | bytes 131096
  5.0 0.0 copy-start.4
  5.0 0.9 %copy-done.4 = f32[2048,16]{0,1:T(8,128)S(1)} copy-done((f32[2048,16]{0,1:T(8,128)S(1)}, f32[2048,16]{0,1:T(8,128)}, u32[]{:S(2)}) %copy-start.4) | copy-done | bytes 131096
  5.9 0.0 copy-start.5
  5.9 0.9 %copy-done.5 = f32[3,3,2048]{2,1,0:T(4,128)S(1)} copy-done((f32[3,3,2048]{2,1,0:T(4,128)S(1)}, f32[3,3,2048]{2,1,0:T(4,128)}, u32[]{:S(2)}) %copy-start.5) | copy-done | bytes 73752
  6.8 0.0 copy-start.6
  6.8 0.7 %copy-done.6 = f32[2048]{0:T(1024)S(1)} copy-done((f32[2048]{0:T(1024)S(1)}, f32[2048]{0:T(1024)}, u32[]{:S(2)}) %copy-start.6) | copy-done | bytes 8216
  7.5 0.0 copy-start.7
  7.5 0.7 %copy-done.7 = s32[2]{0:T(128)S(1)} copy-done((s32[2]{0:T(128)S(1)}, s32[2]{0:T(128)}, u32[]{:S(2)}) %copy-start.7) | copy-done | bytes 32
  8.2 51.5 %shard_map.95 = (bf16[128,2048]{1,0:T(8,128)(2,1)S(1)}, bf16[128,2048]{1,0:T(8,128)(2,1)S(1)}) custom-call(s32[2]{0:T(128)S(1)} %copy-done.7, bf16[3,128,2048]{2,1,0:T(8,128)(2,1)S(1)} %copy-done, f32[3,3,2048]{2,1,0:T(4,128)S(1)} %copy-done.5, f32[16,2048]{1,0:T(8,128)S(1)} %bitcast.3, f32[16,2048]{1,0:T(8,128)S(1)} %bitcast.4, f32[1,2048]{1,0:T(1,128)S(1)} %bitcast.5, ...), custom_call_target="tpu_custom_call" | custom-call | flops 402653184 | bytes 3670016 | tf_op jit(solution)/shard_map/pallas_call | solution.py:545
  59.7 0.8 %copy.12 = bf16[128,2048]{1,0:T(8,128)(2,1)} copy(bf16[128,2048]{1,0:T(8,128)(2,1)S(1)} %get-tuple-element.4) | data formatting | bytes 1048576
  60.5 0.8 %copy.13 = bf16[128,2048]{1,0:T(8,128)(2,1)} copy(bf16[128,2048]{1,0:T(8,128)(2,1)S(1)} %get-tuple-element.5) | data formatting | bytes 1048576
Async XLA Ops:
  0.6 1.4 %copy-start = (bf16[3,128,2048]{2,1,0:T(8,128)(2,1)S(1)}, bf16[3,128,2048]{2,1,0:T(8,128)(2,1)}, u32[]{:S(2)}) copy-start(bf16[3,128,2048]{2,1,0:T(8,128)(2,1)} %streams.1) | copy-start | bytes 4718596
  2.0 1.0 %copy-start.1 = (bf16[128,2048]{1,0:T(8,128)(2,1)S(1)}, bf16[128,2048]{1,0:T(8,128)(2,1)}, u32[]{:S(2)}) copy-start(bf16[128,2048]{1,0:T(8,128)(2,1)} %queries.1) | copy-start | bytes 1572868
  3.1 1.0 %copy-start.2 = (bf16[128,2048]{1,0:T(8,128)(2,1)S(1)}, bf16[128,2048]{1,0:T(8,128)(2,1)}, u32[]{:S(2)}) copy-start(bf16[128,2048]{1,0:T(8,128)(2,1)} %keys.1) | copy-start | bytes 1572868
  4.1 0.9 %copy-start.3 = (f32[2048,16]{0,1:T(8,128)S(1)}, f32[2048,16]{0,1:T(8,128)}, u32[]{:S(2)}) copy-start(f32[2048,16]{0,1:T(8,128)} %param.10) | copy-start | bytes 393220
  5.0 0.9 %copy-start.4 = (f32[2048,16]{0,1:T(8,128)S(1)}, f32[2048,16]{0,1:T(8,128)}, u32[]{:S(2)}) copy-start(f32[2048,16]{0,1:T(8,128)} %param.11) | copy-start | bytes 393220
  5.9 0.9 %copy-start.5 = (f32[3,3,2048]{2,1,0:T(4,128)S(1)}, f32[3,3,2048]{2,1,0:T(4,128)}, u32[]{:S(2)}) copy-start(f32[3,3,2048]{2,1,0:T(4,128)} %taps.1) | copy-start | bytes 221188
  6.8 0.7 %copy-start.6 = (f32[2048]{0:T(1024)S(1)}, f32[2048]{0:T(1024)}, u32[]{:S(2)}) copy-start(f32[2048]{0:T(1024)} %param.12) | copy-start | bytes 24580
  7.5 0.7 %copy-start.7 = (s32[2]{0:T(128)S(1)}, s32[2]{0:T(128)}, u32[]{:S(2)}) copy-start(s32[2]{0:T(128)} %lengths.1) | copy-start | bytes 28

commit v2 on v1

--- a/solution.py
+++ b/solution.py
@@ -176,11 +176,11 @@
 
 
 def fused_kernel(
-    lengths, streams, taps, rate, residue, skip, queries, keys, hyena, attended,
-    ext, rim_out, rim_in, same, mixed_seg, gate_seg, starts, own, own_low, state_in, incoming,
+    lengths, streams_far, taps_far, rate_far, residue_far, skip_far, queries_far, keys_far,
+    hyena, attended, streams, taps, rate, residue, skip, queries, keys, ext, rim_out, rim_in, same, mixed_seg, gate_seg, starts, own, own_low, state_in, incoming,
     tokens, query_in, key_in, value_in, part_out, part_in, lse_out, lse_in, own_part, lse_rows, bias,
     rim_s, rim_r, state_s, state_r, query_s, query_r, key_s, key_r, value_s, value_r,
-    part_s, part_r, lse_s, lse_r,
+    part_s, part_r, lse_s, lse_r, load_s,
 ):
     me = lax.axis_index("ctx")
     rows, width = queries.shape
@@ -203,17 +203,20 @@
     def rim_copy(to):
         return send(rim_out, rim_in, rim_s, rim_r, to)
 
-    def state_copy(source, to):
-        return send(own_low, state_in.at[source], state_s.at[to], state_r.at[source], to)
+    def state_copy(source, g, to):
+        return send(
+            own_low.at[:, cols(g)], state_in.at[source, :, cols(g)],
+            state_s.at[to, g], state_r.at[source, g], to,
+        )
 
     def query_copy(slot, g, to):
         return send(
-            queries.at[:, cols(g)], query_in.at[slot, :, cols(g)],
+            queries_far.at[:, cols(g)], query_in.at[slot, :, cols(g)],
             query_s.at[to, g], query_r.at[slot, g], to,
         )
 
     def key_copy(g):
-        return send(keys.at[:, cols(g)], key_in.at[:, cols(g)], key_s.at[g], key_r.at[g], 1)
+        return send(keys_far.at[:, cols(g)], key_in.at[:, cols(g)], key_s.at[g], key_r.at[g], 1)
 
     def value_copy(g):
         return send(hyena.at[:, cols(g)], value_in.at[:, cols(g)], value_s.at[g], value_r.at[g], 1)
@@ -224,8 +227,18 @@
             part_s.at[slot, g], part_r.at[source - 1, g], to,
         )
 
-    def lse_copy(slot, source, to):
-        return send(lse_out.at[slot], lse_in.at[source - 1], lse_s.at[slot], lse_r.at[source - 1], to)
+    def lse_copy(slot, source, g, to):
+        return send(
+            lse_out.at[slot, g], lse_in.at[source - 1, g], lse_s.at[slot, g], lse_r.at[source - 1, g], to
+        )
+
+    pairs = (
+        (streams_far, streams), (rate_far, rate), (taps_far, taps), (residue_far, residue),
+        (skip_far, skip), (keys_far, keys), (queries_far, queries),
+    )
+    loads = [pltpu.make_async_copy(far, near, load_s.at[n]) for n, (far, near) in enumerate(pairs)]
+    for load in loads:
+        load.start()
 
     barrier = pltpu.get_barrier_semaphore()
     for away in range(1, 4):
@@ -233,6 +246,7 @@
             barrier, inc=1, device_id={"ctx": lax.rem(me + away, 4)},
             device_id_type=pl.DeviceIdType.MESH,
         )
+    loads[0].wait()
     for j in range(3):
         rim_out[2 * j : 2 * j + 2, :] = streams[j, rows - 16 :, :].astype(jnp.float32)[14:16]
     rim_out[6:8, :] = jnp.zeros((2, width), jnp.float32)
@@ -286,29 +300,25 @@
     before = segment * 0 + (first - 1)
     carried = equal(first + segment * seg - 1, before)
 
-    def widen(h, _):
+    @pl.when(me == 0)
+    def _():
+        rim_in[...] = jnp.zeros(rim_in.shape, jnp.float32)
+
+    for i in range(1, 4):
+        @pl.when(me == i)
+        def _():
+            rim_copy(i - 1).wait_recv()
+
+    for load in loads[1:]:
+        load.wait()
+
+    def spread(value):
+        return jnp.broadcast_to(value[:, None, :], (modes, SEGS, LANES))
+
+    def forward(h, _):
         lanes = pl.ds(pl.multiple_of(h * LANES, LANES), LANES)
         for j in range(3):
             ext[j, h, 8:, :] = streams[j, :, lanes].astype(jnp.float32)
-        return _
-
-    lax.fori_loop(0, heads, widen, 0)
-
-    @pl.when(me == 0)
-    def _():
-        rim_in[...] = jnp.zeros(rim_in.shape, jnp.float32)
-
-    for i in range(1, 4):
-        @pl.when(me == i)
-        def _():
-            rim_copy(i - 1).wait_recv()
-
-    def spread(value):
-        return jnp.broadcast_to(value[:, None, :], (modes, SEGS, LANES))
-
-    def forward(h, _):
-        lanes = pl.ds(pl.multiple_of(h * LANES, LANES), LANES)
-        for j in range(3):
             ext[j, h, 6:8, :] = rim_in[2 * j : 2 * j + 2, lanes]
         speed = rate[:, lanes]
         decay = spread(jnp.exp(-speed))
@@ -339,32 +349,36 @@
         starts[h] = pltpu.roll(state, 1, 1) * (segment >= 1).astype(jnp.float32)[None]
         return _
 
-    lax.fori_loop(0, heads, forward, 0)
-    own_low[...] = own[...].astype(jnp.bfloat16)
-    for i in range(3):
-        @pl.when(me == i)
-        def _():
-            for to in range(i + 1, 4):
-                state_copy(i, to).start()
-
-    incoming[...] = jnp.zeros(incoming.shape, jnp.float32)
     edge = jnp.zeros((1, LANES), jnp.int32)
-    for i in range(1, 4):
-        @pl.when(me == i)
-        def _():
-            for j in range(i - 1, -1, -1):
-                state_copy(j, i).wait_recv()
-                linked = equal(edge + (j + 1) * rows - 1, edge + i * rows - 1)
-                linked = jnp.concatenate([linked] * heads, axis=1)
-                span = jnp.exp(-rate[...] * float(rows * (i - 1 - j))) * linked
-                incoming[...] = incoming[...] + state_in[j].astype(jnp.float32) * span
+
+    def forward_group(g):
+        lax.fori_loop(g * per, (g + 1) * per, forward, 0)
+        own_low[:, cols(g)] = own[:, cols(g)].astype(jnp.bfloat16)
+        for i in range(3):
+            @pl.when(me == i)
+            def _():
+                for to in range(i + 1, 4):
+                    state_copy(i, g, to).start()
+
+    def receive_group(g):
+        incoming[:, cols(g)] = jnp.zeros((modes, group), jnp.float32)
+        for i in range(1, 4):
+            @pl.when(me == i)
+            def _():
+                for j in range(i - 1, -1, -1):
+                    state_copy(j, g, i).wait_recv()
+                    linked = equal(edge + (j + 1) * rows - 1, edge + i * rows - 1)
+                    linked = jnp.concatenate([linked] * per, axis=1)
+                    span = jnp.exp(-rate[:, cols(g)] * float(rows * (i - 1 - j))) * linked
+                    arrived = state_in[j, :, cols(g)].astype(jnp.float32)
+                    incoming[:, cols(g)] = incoming[:, cols(g)] + arrived * span
 
     age = (segment * seg).astype(jnp.float32)
 
     def backward(h, _):
         lanes = pl.ds(pl.multiple_of(h * LANES, LANES), LANES)
         speed = spread(rate[:, lanes])
-        decay = jnp.exp(-speed)
+        decay = spread(jnp.exp(-rate[:, lanes]))
         weight = spread(residue[:, lanes])
         direct = jnp.broadcast_to(skip[:, lanes], (SEGS, LANES))
         state = starts[h] + spread(incoming[:, lanes]) * (jnp.exp(-speed * age[None]) * carried[None])
@@ -376,13 +390,6 @@
         hyena[:, lanes] = tokens[...].astype(jnp.bfloat16)
         return _
 
-    for g in range(PARTS):
-        lax.fori_loop(g * per, (g + 1) * per, backward, 0)
-
-        @pl.when(me == 0)
-        def _():
-            value_copy(g).start()
-
     scale = 1.0 / math.sqrt(HEAD_DIM)
     lane = lax.broadcasted_iota(jnp.int32, (rows, LANES), 1)
     down = lax.broadcasted_iota(jnp.int32, (rows, rows), 0)
@@ -404,124 +411,146 @@
         summed = jnp.dot(weight.astype(jnp.bfloat16), value, preferred_element_type=jnp.float32)
         return summed * (1.0 / total), top + jnp.log(total)
 
-    def note(slot, h, value):
-        lse_rows[slot] = jnp.where(lane == h, value, lse_rows[slot])
+    def note(slot, g, h, value):
+        lse_rows[slot, g] = jnp.where(lane == h - g * per, value, lse_rows[slot, g])
+
+    def send_part(slot, source, g, to, table):
+        lse_out[slot, g] = lse_rows[table, g].T[:SEGS]
+        lse_copy(slot, source, g, to).start()
+        part_copy(slot, source, g, to).start()
 
     def head_lanes(h):
         return pl.ds(pl.multiple_of(h * LANES, LANES), LANES)
 
-    def combine(sources):
-        tables = [lse_rows[0]]
+    def attend_own(h, _):
+        at = head_lanes(h)
+        out, lse = attend(queries[:, at], keys[:, at], hyena[:, at], bias[:rows, :rows])
+        attended[:, at] = out.astype(jnp.bfloat16)
+        return _
+
+    def attend_second(g, h, _):
+        at = head_lanes(h)
+        query = jnp.concatenate([query_in[0, :, at], query_in[1, :, at], queries[:, at]], axis=0)
+        key = jnp.concatenate([key_in[:, at], keys[:, at]], axis=0)
+        value = jnp.concatenate([value_in[:, at], hyena[:, at]], axis=0)
+        out, lse = attend(query, key, value, bias[...])
+        part_out[0, :, at] = out[:rows].astype(jnp.bfloat16)
+        part_out[1, :, at] = out[rows : 2 * rows].astype(jnp.bfloat16)
+        attended[:, at] = out[2 * rows :].astype(jnp.bfloat16)
+        note(0, g, h, lse[:rows])
+        note(1, g, h, lse[rows : 2 * rows])
+        return _
+
+    def attend_third(g, h, _):
+        at = head_lanes(h)
+        query = jnp.concatenate([query_in[1, :, at], queries[:, at]], axis=0)
+        out, lse = attend(query, keys[:, at], hyena[:, at], bias[: 2 * rows, :rows])
+        part_out[0, :, at] = out[:rows].astype(jnp.bfloat16)
+        own_part[:, at] = out[rows:]
+        note(1, g, h, lse[:rows])
+        note(0, g, h, lse[rows:])
+        return _
+
+    def attend_last(g, h, _):
+        at = head_lanes(h)
+        out, lse = attend(queries[:, at], keys[:, at], hyena[:, at], bias[:rows, :rows])
+        own_part[:, at] = out
+        note(0, g, h, lse)
+        return _
+
+    def combine(sources, g):
+        tables = [lse_rows[0, g]]
         for source in sources:
-            lse_copy(0, source, 0).wait_recv()
-            filler = jnp.zeros((LANES - heads, rows), jnp.float32)
-            tables.append(jnp.concatenate([lse_in[source - 1], filler], axis=0).T)
+            lse_copy(0, source, g, 0).wait_recv()
+            filler = jnp.zeros((LANES - SEGS, rows), jnp.float32)
+            tables.append(jnp.concatenate([lse_in[source - 1, g], filler], axis=0).T)
         peak = functools.reduce(jnp.maximum, tables)
         shares = [jnp.exp(table - peak) for table in tables]
         norm = 1.0 / functools.reduce(jnp.add, shares)
         shares = [share * norm for share in shares]
-        for g in range(PARTS):
-            for source in sources:
-                part_copy(0, source, g, 0).wait_recv()
-            for h in range(g * per, (g + 1) * per):
-                at = slice(h * LANES, (h + 1) * LANES)
-                whole = own_part[:, at] * shares[0][:, h : h + 1]
-                for share, source in zip(shares[1:], sources):
-                    whole = whole + part_in[source - 1, :, at].astype(jnp.float32) * share[:, h : h + 1]
-                attended[:, at] = whole.astype(jnp.bfloat16)
+        for source in sources:
+            part_copy(0, source, g, 0).wait_recv()
+        for n in range(per):
+            at = slice((g * per + n) * LANES, (g * per + n + 1) * LANES)
+            whole = own_part[:, at] * shares[0][:, n : n + 1]
+            for share, source in zip(shares[1:], sources):
+                whole = whole + part_in[source - 1, :, at].astype(jnp.float32) * share[:, n : n + 1]
+            attended[:, at] = whole.astype(jnp.bfloat16)
 
     @pl.when(me == 0)
     def _():
         set_bias(0, 0, 0, 0)
 
-        def one(h, _):
-            at = head_lanes(h)
-            out, lse = attend(queries[:, at], keys[:, at], hyena[:, at], bias[:rows, :rows])
-            attended[:, at] = out.astype(jnp.bfloat16)
-            return _
-
-        lax.fori_loop(0, heads, one, 0)
-        for g in range(PARTS):
-            key_copy(g).wait_send()
-            value_copy(g).wait_send()
-
     @pl.when(me == 1)
     def _():
-        for a in range(3):
+        for a, query_block in enumerate((2, 3, 1)):
             for b in range(2):
-                set_bias(a + 1, b, a, b)
-
-        def one(h, _):
-            at = head_lanes(h)
-            query = jnp.concatenate([query_in[0, :, at], query_in[1, :, at], queries[:, at]], axis=0)
-            key = jnp.concatenate([key_in[:, at], keys[:, at]], axis=0)
-            value = jnp.concatenate([value_in[:, at], hyena[:, at]], axis=0)
-            penalty = jnp.concatenate([bias[rows:, :], bias[:rows, :]], axis=0)
-            out, lse = attend(query, key, value, penalty)
-            part_out[0, :, at] = out[:rows].astype(jnp.bfloat16)
-            part_out[1, :, at] = out[rows : 2 * rows].astype(jnp.bfloat16)
-            attended[:, at] = out[2 * rows :].astype(jnp.bfloat16)
-            note(0, h, lse[:rows])
-            note(1, h, lse[rows : 2 * rows])
-            return _
-
-        for g in range(PARTS):
+                set_bias(query_block, b, a, b)
+
+    @pl.when(me == 2)
+    def _():
+        set_bias(3, 2, 0, 0)
+        set_bias(2, 2, 1, 0)
+
+    @pl.when(me == 3)
+    def _():
+        set_bias(3, 3, 0, 0)
+
+    forward_group(0)
+    for g in range(PARTS):
+        if g + 1 < PARTS:
+            forward_group(g + 1)
+        receive_group(g)
+        lo, hi = g * per, (g + 1) * per
+        lax.fori_loop(lo, hi, backward, 0)
+
+        @pl.when(me == 0)
+        def _():
+            value_copy(g).start()
+            lax.fori_loop(lo, hi, attend_own, 0)
+
+        @pl.when(me == 1)
+        def _():
             query_copy(0, g, 1).wait_recv()
             query_copy(1, g, 1).wait_recv()
             key_copy(g).wait_recv()
             value_copy(g).wait_recv()
-            lax.fori_loop(g * per, (g + 1) * per, one, 0)
-            part_copy(0, 1, g, 2).start()
-            part_copy(1, 1, g, 3).start()
-        for slot in range(2):
-            lse_out[slot] = lse_rows[slot].T[:heads]
-            lse_copy(slot, 1, slot + 2).start()
-        for slot in range(2):
-            for g in range(PARTS):
+            lax.fori_loop(lo, hi, functools.partial(attend_second, g), 0)
+            send_part(0, 1, g, 2, 0)
+            send_part(1, 1, g, 3, 1)
+
+        @pl.when(me == 2)
+        def _():
+            query_copy(1, g, 2).wait_recv()
+            lax.fori_loop(lo, hi, functools.partial(attend_third, g), 0)
+            send_part(0, 2, g, 3, 1)
+
+        @pl.when(me == 3)
+        def _():
+            lax.fori_loop(lo, hi, functools.partial(attend_last, g), 0)
+
+    for g in range(PARTS):
+        @pl.when(me == 0)
+        def _():
+            key_copy(g).wait_send()
+            value_copy(g).wait_send()
+
+        @pl.when(me == 1)
+        def _():
+            for slot in range(2):
                 part_copy(slot, 1, g, slot + 2).wait_send()
-            lse_copy(slot, 1, slot + 2).wait_send()
-
-    @pl.when(me == 2)
-    def _():
-        set_bias(3, 2, 0, 0)
-        set_bias(2, 2, 1, 0)
-
-        def one(h, _):
-            at = head_lanes(h)
-            query = jnp.concatenate([query_in[1, :, at], queries[:, at]], axis=0)
-            out, lse = attend(query, keys[:, at], hyena[:, at], bias[: 2 * rows, :rows])
-            part_out[0, :, at] = out[:rows].astype(jnp.bfloat16)
-            own_part[:, at] = out[rows:]
-            note(1, h, lse[:rows])
-            note(0, h, lse[rows:])
-            return _
-
-        for g in range(PARTS):
-            query_copy(1, g, 2).wait_recv()
-            lax.fori_loop(g * per, (g + 1) * per, one, 0)
-            part_copy(0, 2, g, 3).start()
-        lse_out[0] = lse_rows[1].T[:heads]
-        lse_copy(0, 2, 3).start()
-        combine((1,))
-        for g in range(PARTS):
+                lse_copy(slot, 1, g, slot + 2).wait_send()
+
+        @pl.when(me == 2)
+        def _():
+            combine((1,), g)
             query_copy(0, g, 1).wait_send()
             part_copy(0, 2, g, 3).wait_send()
-        lse_copy(0, 2, 3).wait_send()
-
-    @pl.when(me == 3)
-    def _():
-        set_bias(3, 3, 0, 0)
-
-        def one(h, _):
-            at = head_lanes(h)
-            out, lse = attend(queries[:, at], keys[:, at], hyena[:, at], bias[:rows, :rows])
-            own_part[:, at] = out
-            note(0, h, lse)
-            return _
-
-        lax.fori_loop(0, heads, one, 0)
-        combine((2, 1))
-        for g in range(PARTS):
+            lse_copy(0, 2, g, 3).wait_send()
+
+        @pl.when(me == 3)
+        def _():
+            combine((2, 1), g)
             query_copy(1, g, 1).wait_send()
             query_copy(1, g, 2).wait_send()
 
@@ -530,7 +559,8 @@
         def _():
             rim_copy(i + 1).wait_send()
             for to in range(i + 1, 4):
-                state_copy(i, to).wait_send()
+                for g in range(PARTS):
+                    state_copy(i, g, to).wait_send()
 
 
 def fused(streams, short_filter, decay_rate, residue, skip_gain, lengths, queries, keys):
@@ -541,13 +571,21 @@
     f32, bf16 = jnp.float32, jnp.bfloat16
     vmem, dma = pltpu.VMEM, pltpu.SemaphoreType.DMA
     block = pl.BlockSpec(memory_space=pltpu.VMEM)
+    far = pl.BlockSpec(memory_space=pltpu.HBM)
     out = jax.ShapeDtypeStruct((rows, width), bf16)
     return pl.pallas_call(
         fused_kernel,
         out_shape=(out, out),
-        in_specs=[pl.BlockSpec(memory_space=pltpu.SMEM)] + [block] * 7,
+        in_specs=[pl.BlockSpec(memory_space=pltpu.SMEM)] + [far] * 7,
         out_specs=(block, block),
         scratch_shapes=[
+            vmem(streams.shape, bf16),
+            vmem(short_filter.shape, f32),
+            vmem((modes, width), f32),
+            vmem((modes, width), f32),
+            vmem((1, width), f32),
+            vmem((rows, width), bf16),
+            vmem((rows, width), bf16),
             vmem((3, heads, rows + 8, LANES), f32),
             vmem((8, width), f32),
             vmem((8, width), f32),
@@ -565,17 +603,17 @@
             vmem((rows, width), bf16),
             vmem((2, rows, width), bf16),
             vmem((2, rows, width), bf16),
-            vmem((2, heads, rows), f32),
-            vmem((2, heads, rows), f32),
+            vmem((2, PARTS, SEGS, rows), f32),
+            vmem((2, PARTS, SEGS, rows), f32),
             vmem((rows, width), f32),
-            vmem((2, rows, LANES), f32),
+            vmem((2, PARTS, rows, LANES), f32),
             vmem((3 * rows, 2 * rows), f32),
-            dma, dma, dma((4,)), dma((3,)), dma((4, PARTS)), dma((2, PARTS)),
+            dma, dma, dma((4, PARTS)), dma((3, PARTS)), dma((4, PARTS)), dma((2, PARTS)),
             dma((PARTS,)), dma((PARTS,)), dma((PARTS,)), dma((PARTS,)),
-            dma((2, PARTS)), dma((2, PARTS)), dma((2,)), dma((2,)),
+            dma((2, PARTS)), dma((2, PARTS)), dma((2, PARTS)), dma((2, PARTS)), dma((7,)),
         ],
         compiler_params=pltpu.CompilerParams(
-            collective_id=0, has_side_effects=True, vmem_limit_bytes=48 * 1024 * 1024
+            collective_id=0, has_side_effects=True, vmem_limit_bytes=60 * 1024 * 1024
         ),
         cost_estimate=pl.CostEstimate(
             flops=12 * rows * rows * width, bytes_accessed=14 * rows * width, transcendentals=0

time: 61.7 us -> 57 us (0.924)
  local copies, waits for them, and re-layouts: 9.12 us -> 3.76 us
  Pallas kernels: 51.5 us -> 52.3 us
    unnamed x18 -> x2, local copies, waits for them, and re-layouts: 9.12 us -> 3.76 us
    pallas_call x1, Pallas kernels: 51.5 us -> 52.3 us  [fused(): pl.pallas_call(fused_kernel, out_shape=(out, out), in_specs=[pl.BlockSpec...]
where the time goes in v2:
time: 57 us; the launch traced here: 56.7 us
  Pallas kernels  52.3 us (92%)
  local copies, waits for them, and re-layouts  3.76 us (7%)
  between operations  0.64 us (1%)
    pallas_call x1, Pallas kernels, fused(): pl.pallas_call(fused_kernel, out_shape=(out, out), in_specs=[pl.BlockSpec...  52.3 us
    unnamed x2, local copies, waits for them, and re-layouts  3.76 us

profile of v2, /device:TPU:26, one launch (start us, length us, event | category | flops | bytes accessed | tf_op | source)
XLA Modules:
  0.0 56.7 jit_solution(12588269718526421811)
XLA Ops:
  0.6 52.3 %shard_map.95 = (bf16[128,2048]{1,0:T(8,128)(2,1)}, bf16[128,2048]{1,0:T(8,128)(2,1)}) custom-call(s32[2]{0:T(128)} %lengths.1, bf16[3,128,2048]{2,1,0:T(8,128)(2,1)} %streams_far.1, f32[3,3,2048]{2,1,0:T(4,128)} %taps_far.1, f32[16,2048]{1,0:T(8,128)} %bitcast.3, f32[16,2048]{1,0:T(8,128)} %bitcast.4, f32[1,2048]{1,0:T(1,128)} %bitcast.5, ...), custom_call_target="tpu_custom_call" | custom-call | flops 402653184 | bytes 3670016 | tf_op jit(solution)/shard_map/pallas_call | solution.py:576
  53.0 1.9 %copy.12 = bf16[128,2048]{1,0:T(8,128)(2,1)} copy(bf16[128,2048]{1,0:T(8,128)(2,1)} %get-tuple-element.4) | data formatting | bytes 1048576
  54.9 1.9 %copy.13 = bf16[128,2048]{1,0:T(8,128)(2,1)} copy(bf16[128,2048]{1,0:T(8,128)(2,1)} %get-tuple-element.5) | data formatting | bytes 1048576

commit v3 on v2

--- a/solution.py
+++ b/solution.py
@@ -420,7 +420,7 @@
         part_copy(slot, source, g, to).start()
 
     def head_lanes(h):
-        return pl.ds(pl.multiple_of(h * LANES, LANES), LANES)
+        return pl.ds(h * LANES, LANES)
 
     def attend_own(h, _):
         at = head_lanes(h)
@@ -507,7 +507,8 @@
         @pl.when(me == 0)
         def _():
             value_copy(g).start()
-            lax.fori_loop(lo, hi, attend_own, 0)
+            for h in range(lo, hi):
+                attend_own(h, 0)
 
         @pl.when(me == 1)
         def _():
@@ -515,19 +516,22 @@
             query_copy(1, g, 1).wait_recv()
             key_copy(g).wait_recv()
             value_copy(g).wait_recv()
-            lax.fori_loop(lo, hi, functools.partial(attend_second, g), 0)
+            for h in range(lo, hi):
+                attend_second(g, h, 0)
             send_part(0, 1, g, 2, 0)
             send_part(1, 1, g, 3, 1)
 
         @pl.when(me == 2)
         def _():
             query_copy(1, g, 2).wait_recv()
-            lax.fori_loop(lo, hi, functools.partial(attend_third, g), 0)
+            for h in range(lo, hi):
+                attend_third(g, h, 0)
             send_part(0, 2, g, 3, 1)
 
         @pl.when(me == 3)
         def _():
-            lax.fori_loop(lo, hi, functools.partial(attend_last, g), 0)
+            for h in range(lo, hi):
+                attend_last(g, h, 0)
 
     for g in range(PARTS):
         @pl.when(me == 0)

time: 57 us -> 56.3 us (0.988)
  Pallas kernels: 52.3 us -> 51.6 us
    pallas_call x1, Pallas kernels: 52.3 us -> 51.6 us  [fused(): pl.pallas_call(fused_kernel, out_shape=(out, out), in_specs=[pl.BlockSpec...]
where the time goes in v3:
time: 56.3 us; the launch traced here: 56 us
  Pallas kernels  51.6 us (92%)
  local copies, waits for them, and re-layouts  3.76 us (7%)
  between operations  0.64 us (1%)
    pallas_call x1, Pallas kernels, fused(): pl.pallas_call(fused_kernel, out_shape=(out, out), in_specs=[pl.BlockSpec...  51.6 us
    unnamed x2, local copies, waits for them, and re-layouts  3.76 us

profile of v3, /device:TPU:26, one launch (start us, length us, event | category | flops | bytes accessed | tf_op | source)
XLA Modules:
  0.0 56.0 jit_solution(12378487828204070411)
XLA Ops:
  0.6 51.6 %shard_map.95 = (bf16[128,2048]{1,0:T(8,128)(2,1)}, bf16[128,2048]{1,0:T(8,128)(2,1)}) custom-call(s32[2]{0:T(128)} %lengths.1, bf16[3,128,2048]{2,1,0:T(8,128)(2,1)} %streams_far.1, f32[3,3,2048]{2,1,0:T(4,128)} %taps_far.1, f32[16,2048]{1,0:T(8,128)} %bitcast.3, f32[16,2048]{1,0:T(8,128)} %bitcast.4, f32[1,2048]{1,0:T(1,128)} %bitcast.5, ...), custom_call_target="tpu_custom_call" | custom-call | flops 402653184 | bytes 3670016 | tf_op jit(solution)/shard_map/pallas_call | solution.py:580
  52.2 1.9 %copy.12 = bf16[128,2048]{1,0:T(8,128)(2,1)} copy(bf16[128,2048]{1,0:T(8,128)(2,1)} %get-tuple-element.4) | data formatting | bytes 1048576
  54.1 1.9 %copy.13 = bf16[128,2048]{1,0:T(8,128)(2,1)} copy(bf16[128,2048]{1,0:T(8,128)(2,1)} %get-tuple-element.5) | data formatting | bytes 1048576
